TPU v7x, 512 devices: a whole 4x4x16 slice. The times are simulated.
512 devices in a mesh: replica: 8 (over z_lo), fsdp: 64 (over y, x, z_hi, core).
Axes of the slice: x: 4, y: 4, z: 16 (z_hi: 2, z_lo: 8; z = z_hi * 8 + z_lo), core: 2. Of those that a mesh axis runs over, the one named last changes fastest.
Arguments:
- activations: bfloat16 [8, 8192, 6144], P('replica', 'fsdp'), may hold values from -0.0625 to 0.0625
- up_cotangent: bfloat16 [8, 8192, 512], P('replica', 'fsdp'), may hold values from -6 to 6
- up_weight: bfloat16 [8, 6144, 512], P('replica', 'fsdp'), may hold values from -0.25 to 0.25
- pseudo_grads: bfloat16 [8, 6144, 384], P('replica', 'fsdp'), may hold values from -6 to 6
- outer_params: float32 [6144, 384], P('fsdp'), may hold values from -6 to 6
- outer_moment: float32 [6144, 384], P('fsdp'), may hold values from -6 to 6
Outputs:
- grad_input: bfloat16 [8, 8192, 6144], P('replica', 'fsdp')
- grad_weight: float32 [8, 6144, 512], P('replica', 'fsdp')
- new_params: float32 [6144, 384], P('fsdp')
- new_moment: float32 [6144, 384], P('fsdp')
All inputs are finite; a program needn't handle non-finite values.
Results may differ from a plain program's by a relative error of at most 0.008.
Values may be sent and summed in bfloat16 or wider, within the bound.
A program may use at most 64 MiB of HBM per device.

v0:
```python
import jax
import jax.numpy as jnp
from jax import lax
from jax.sharding import PartitionSpec as P

outer_rate = 0.7
outer_beta = 0.9


def body(activations, up_cotangent, up_weight, pseudo_grads, outer_params, outer_moment):
    own_tokens = activations[0]
    own_cotangent = up_cotangent[0]
    own_rows = up_weight[0]
    columns = lax.all_to_all(own_tokens, "fsdp", split_axis=1, concat_axis=0, tiled=True)
    all_cotangent = lax.all_gather(own_cotangent, "fsdp", axis=0, tiled=True)
    grad_weight = lax.dot_general(
        columns, all_cotangent, (((0,), (0,)), ((), ())), preferred_element_type=jnp.float32
    )
    grad_input = lax.dot_general(
        own_cotangent,
        lax.all_gather(own_rows, "fsdp", axis=0, tiled=True),
        (((1,), (1,)), ((), ())),
        preferred_element_type=jnp.float32,
    ).astype(jnp.bfloat16)
    groups = lax.axis_size("replica")
    total = lax.psum(pseudo_grads[0].astype(jnp.float32).astype(jnp.bfloat16), "replica").astype(
        jnp.float32
    )
    average = total / groups
    new_moment = outer_beta * outer_moment + average
    new_params = outer_params - outer_rate * (average + outer_beta * new_moment)
    return (grad_input[None], grad_weight[None], new_params, new_moment)


def solution(mesh):
    placed = (
        P("replica", "fsdp", None),
        P("replica", "fsdp", None),
        P("replica", "fsdp", None),
        P("replica", "fsdp", None),
        P("fsdp", None),
        P("fsdp", None),
    )
    return jax.shard_map(
        body,
        mesh=mesh,
        in_specs=placed,
        out_specs=(
            P("replica", "fsdp", None),
            P("replica", "fsdp", None),
            P("fsdp", None),
            P("fsdp", None),
        ),
        check_vma=False,
    )
```

profile of v0, /device:TPU:1, one launch (start us, length us, event | category | flops | bytes accessed | tf_op | source)
XLA Modules:
  0.0 390.0 jit_solution(14055193459932763153)
XLA Ops:
  8.0 0.0 all-reduce.2.cloned.1.call-start
  8.0 0.7 all-reduce.2.cloned.1.call-update
  8.7 0.0 all-gather.5.cloned.1.call-start
  8.8 0.5 all-gather.5.cloned.1.call-update
  9.3 0.0 all-gather.7.cloned.1.call-start
  9.4 0.5 all-gather.7.cloned.1.call-update
  9.9 2.6 copy.10
  12.5 0.0 copy-start.1
  12.5 0.0 copy-start.2
  12.5 0.0 copy-start
  12.5 22.4 %all-to-all-start = ((bf16[128,64,96]{0,2,1:T(8,128)(2,1)}), bf16[128,64,96]{0,2,1:T(8,128)(2,1)S(1)}, u32[]{:S(2)}, u32[]{:S(2)}) async-start(bf16[128,64,96]{0,2,1:T(8,128)(2,1)} %bitcast.3), calls=%async_computation | async-start | bytes 3145728 | tf_op jit(solution)/shard_map/all_to_all | solution.py:14
  34.9 180.0 %all-reduce.2.cloned.1.call-done = bf16[96,384]{1,0:T(8,128)(2,1)} async-done(((bf16[96,384]{1,0:T(8,128)(2,1)}), bf16[96,384]{1,0:T(8,128)(2,1)}) %all-reduce.2.cloned.1.call-update) | async-done | bytes 73744 | tf_op jit(solution)/shard_map/psum | solution.py:26
  215.0 0.0 copy-done.1
  215.0 0.0 copy-done.2
  215.0 1.6 multiply_subtract_fusion
  216.6 1.1 all-gather.5.cloned.1.call-done
  217.7 0.0 copy-done
  217.7 6.1 %fusion.2 = bf16[1,128,6144]{2,1,0:T(8,128)(2,1)} fusion(bf16[1,6144,512]{2,1,0:T(8,128)(2,1)} %all-gather.5.cloned.1.call-done, bf16[1,128,512]{2,1,0:T(8,128)(2,1)S(1)} %copy-done), kind=kOutput, calls=%fused_computation.3 | convolution fusion | flops 806092800 | bytes 7995392 | tf_op jit(solution)/shard_map/dot_general | solution.py:19
  223.7 0.0 all-to-all-done
  223.7 153.3 %all-gather.7.cloned.1.call-done = bf16[1,8192,512]{2,1,0:T(8,128)(2,1)} async-done(((bf16[1,128,512]{2,1,0:T(8,128)(2,1)}), bf16[1,8192,512]{2,1,0:T(8,128)(2,1)}) %all-gather.7.cloned.1.call-update) | async-done | bytes 8388624 | tf_op jit(solution)/shard_map/all_gather | solution.py:15
  377.1 5.5 %fusion.6 = f32[1,96,512]{2,1,0:T(8,128)} fusion(bf16[1,8192,512]{2,1,0:T(8,128)(2,1)} %all-gather.7.cloned.1.call-done, bf16[128,64,96]{0,2,1:T(8,128)(2,1)S(1)} %all-to-all-done), kind=kOutput, calls=%fused_computation.7 | convolution fusion | flops 805306368 | bytes 10158080 | tf_op jit(solution)/shard_map/dot_general | solution.py:16
Async XLA Ops:
  8.0 207.0 %all-reduce.2.cloned.1.call-start = ((), (), s32[]{:S(2)}) async-start(), calls=%async_computation.1 | async-start | bytes 147456 | tf_op jit(solution)/shard_map/psum | solution.py:26
  8.7 208.9 %all-gather.5.cloned.1.call-start = ((), (), s32[]{:S(2)}) async-start(), calls=%async_computation.2 | async-start | bytes 6389760 | tf_op jit(solution)/shard_map/all_gather | solution.py:21
  9.3 367.8 %all-gather.7.cloned.1.call-start = ((), (), s32[]{:S(2)}) async-start(), calls=%async_computation.3 | async-start | bytes 8519680 | tf_op jit(solution)/shard_map/all_gather | solution.py:15
  12.5 202.4 %copy-start.1 = (f32[96,384]{1,0:T(8,128)S(1)}, f32[96,384]{1,0:T(8,128)}, u32[]{:S(2)}) copy-start(f32[96,384]{1,0:T(8,128)} %param.10) | copy-start | bytes 442372
  12.5 202.4 %copy-start.2 = (f32[96,384]{1,0:T(8,128)S(1)}, f32[96,384]{1,0:T(8,128)}, u32[]{:S(2)}) copy-start(f32[96,384]{1,0:T(8,128)} %param.11) | copy-start | bytes 442372
  12.5 205.1 %copy-start = (bf16[1,128,512]{2,1,0:T(8,128)(2,1)S(1)}, bf16[1,128,512]{2,1,0:T(8,128)(2,1)}, u32[]{:S(2)}) copy-start(bf16[1,128,512]{2,1,0:T(8,128)(2,1)} %param.7) | copy-start | bytes 393220
  12.5 211.2 %all-to-all-start = ((bf16[128,64,96]{0,2,1:T(8,128)(2,1)}), bf16[128,64,96]{0,2,1:T(8,128)(2,1)S(1)}, u32[]{:S(2)}, u32[]{:S(2)}) async-start(bf16[128,64,96]{0,2,1:T(8,128)(2,1)} %bitcast.3), calls=%async_computation | async-start | bytes 3145728 | tf_op jit(solution)/shard_map/all_to_all | solution.py:14
Sparse Core Ops, SparseCore 0:
  11.7 203.1 all-reduce.1
Sparse Core Ops, SparseCore 1:
  13.6 204.0 all-gather.4
  221.9 155.1 all-gather.6
where the time goes:
time: 394 us; the launch traced here: 390 us
  waiting for transfers between devices  336 us (85%)
  starting transfers between devices  22.5 us (6%)
  between operations  15.5 us (4%)
  matrix products  11.6 us (3%)
    psum x1, waiting for transfers between devices, body(): lax.psum(pseudo_grads[0].astype(jnp.float32).astype(jnp.bfloat16), 'repli...  180 us
    all_gather x1, waiting for transfers between devices, body(): all_cotangent = lax.all_gather(own_cotangent, 'fsdp', axis=0, tiled=True)  153 us
    all_to_all x1, starting transfers between devices, body(): lax.all_to_all(own_tokens, 'fsdp', split_axis=1, concat_axis=0, tiled=True)  22.4 us
  transfers between devices with their start and end apart: 4, of which 3 were waited for; matrix products, arithmetic and copies ran while one was open for 3% of the time, Pallas kernels for 0%

commit v1 on v0

v1 whole, which is shorter than its diff:
```python
import jax
import jax.numpy as jnp
from jax import lax
from jax.experimental import pallas as pl
from jax.experimental.pallas import tpu as pltpu
from jax.sharding import PartitionSpec as P

outer_rate = 0.7
outer_beta = 0.9

SIDE = 4
GROUPS = 8
TOK = 128
ROWS = 96
D = 6144
FW = 512
HALF = FW // 2
PART = HALF // 2
BLOCK = 4 * ROWS
FRAG = 384
CUT = ROWS // GROUPS
PAD = 16
HROWS = ROWS // 2

MESH = pl.DeviceIdType.MESH
ORDER = (1, 3, 2)


def kernel(
    act, cot, weight, pseudo, params, moment,
    gi_out, gw_out, params_out, moment_out,
    a_buf, c_buf, ct_buf, p_x, p_y, r_x, r_y, s_x, s_y, q_x, q_y, total, z_src, z_dst, swap, gw_buf,
    w_buf, gi_buf, g_buf, g_wide, g_src, g_dst, h_src, h_dst, par_buf, mom_buf,
    load_sem, store_sem, core_send, core_recv, rs_send, rs_recv, z_send, z_recv,
    w1_send, w1_recv, w2_send, w2_recv, wc_send, wc_recv, g_send, g_recv, h_send, h_recv,
):
    r = lax.axis_index("replica")
    f = lax.axis_index("fsdp")
    y, x, zh, c = f // 16, (f // 4) % 4, (f // 2) % 2, f % 2

    def at(y, x, zh, c):
        return (r, ((y * 4 + x) * 2 + zh) * 2 + c)

    def along_x(k):
        return at(y, (x + k) % 4, zh, c)

    def along_y(k):
        return at((y + k) % 4, x, zh, c)

    def along_r(k):
        return ((r + k) % GROUPS, f)

    peer = at(y, x, zh, 1 - c)
    across = at(y, x, 1 - zh, c)

    sent = []

    def send(src, dst, ss, rs, to):
        copy = pltpu.make_async_remote_copy(
            src_ref=src, dst_ref=dst, send_sem=ss, recv_sem=rs, device_id=to, device_id_type=MESH
        )
        copy.start()
        sent.append(copy)
        return copy

    own_w = w_buf.at[y, x, pl.ds(pl.multiple_of((zh * 2 + c) * ROWS, ROWS), ROWS)]
    loads = [
        pltpu.make_async_copy(weight, own_w, load_sem.at[0]),
        pltpu.make_async_copy(cot, c_buf.at[0], load_sem.at[1]),
        pltpu.make_async_copy(act, a_buf.at[pl.ds(0, TOK)], load_sem.at[2]),
        pltpu.make_async_copy(pseudo, g_buf, load_sem.at[3]),
        pltpu.make_async_copy(params, par_buf, load_sem.at[4]),
        pltpu.make_async_copy(moment, mom_buf, load_sem.at[5]),
    ]
    for copy in loads:
        copy.start()

    barrier = pltpu.get_barrier_semaphore()
    friends = [peer, across]
    friends += [along_x(k) for k in ORDER] + [along_y(k) for k in ORDER]
    friends += [along_r(k) for k in range(1, GROUPS)]
    for to in friends:
        pl.semaphore_signal(barrier, inc=1, device_id=to, device_id_type=MESH)

    loads[3].wait()
    g_wide[...] = g_buf[...].astype(jnp.float32)
    for j in range(GROUPS):
        g_src[j, 0:CUT, :] = g_wide[j * CUT:(j + 1) * CUT, :]
        g_src[j, CUT:PAD, :] = jnp.zeros((PAD - CUT, FRAG), jnp.float32)
    for j in range(GROUPS):
        h_src[j] = g_src[j].astype(jnp.bfloat16)
    loads[0].wait()
    loads[1].wait()
    loads[2].wait()
    pl.semaphore_wait(barrier, len(friends))

    z_w = send(own_w, own_w, z_send.at[0], z_recv.at[0], across)
    c_copy = send(c_buf.at[0], c_buf.at[1], core_send.at[0], core_recv.at[0], peer)
    a_copies = []
    for i, k in enumerate((1, 3, 2, 0)):
        cols = pl.ds(pl.multiple_of(((y + k) % 4) * (4 * BLOCK), 128), 4 * BLOCK)
        a_copies.append(
            send(
                a_buf.at[pl.ds(0, TOK), cols], a_buf.at[pl.ds(TOK, TOK), cols],
                core_send.at[1 + i], core_recv.at[1 + i], peer,
            )
        )

    def w_rows(plane, second):
        return pl.ds(pl.multiple_of((plane * 2 + c) * ROWS + second * HROWS, 16), HROWS)

    def w_first(s, plane):
        copies = []
        for k in ORDER:
            ref = w_buf.at[y, x, w_rows(plane, 0)]
            copies.append(send(ref, ref, w1_send.at[s, 0, k - 1], w1_recv.at[s, 0, k - 1], along_x(k)))
            ref = w_buf.at[y, x, w_rows(plane, 1)]
            copies.append(send(ref, ref, w1_send.at[s, 1, k - 1], w1_recv.at[s, 1, k - 1], along_y(k)))
        return copies

    def w_second(s, plane):
        copies = []
        for k in ORDER:
            ref = w_buf.at[y, :, w_rows(plane, 0)]
            copies.append(send(ref, ref, w2_send.at[s, 0, k - 1], w2_recv.at[s, 0, k - 1], along_y(k)))
            ref = w_buf.at[:, x, w_rows(plane, 1)]
            copies.append(send(ref, ref, w2_send.at[s, 1, k - 1], w2_recv.at[s, 1, k - 1], along_x(k)))
        return copies

    def w_core(s, plane, k):
        ref = w_buf.at[(y - k) % 4, :, w_rows(plane, 0)]
        one = send(ref, ref, wc_send.at[s, 0, k], wc_recv.at[s, 0, k], peer)
        ref = w_buf.at[:, (x - k) % 4, w_rows(plane, 1)]
        two = send(ref, ref, wc_send.at[s, 1, k], wc_recv.at[s, 1, k], peer)
        return [one, two]

    w1_own = w_first(0, zh)

    g_copies = []
    for k in range(1, GROUPS):
        g_copies.append(
            send(h_src.at[(r + k) % GROUPS], g_dst.at[k], g_send.at[k], g_recv.at[k], along_r(k))
        )

    c_copy.wait_recv()
    mine = pl.ds(pl.multiple_of(c * HALF, HALF), HALF)
    ct_buf[:, 0:TOK] = c_buf[0, :, mine].T
    ct_buf[:, TOK:2 * TOK] = c_buf[1, :, mine].T
    rs_copies_y = []
    for i, k in enumerate((1, 3, 2, 0)):
        a_copies[i].wait_recv()

        def block(j, _, k=k):
            col = pl.multiple_of((((y + k) % 4) * 4 + (x + j) % 4) * BLOCK, 128)
            part = jnp.dot(ct_buf[...], a_buf[:, pl.ds(col, BLOCK)], preferred_element_type=jnp.float32)
            part = part.astype(jnp.bfloat16)
            p_x[j, k] = part[0:PART]
            p_y[k, j] = part[PART:HALF]
            return 0

        lax.fori_loop(0, 4, block, 0)
        if k:
            rs_copies_y.append(
                send(p_y.at[k], r_y.at[k - 1], rs_send.at[0, 1, k - 1], rs_recv.at[0, 1, k - 1], along_y(k))
            )
    rs_copies_x = [
        send(p_x.at[k], r_x.at[k - 1], rs_send.at[0, 0, k - 1], rs_recv.at[0, 0, k - 1], along_x(k)) for k in ORDER
    ]

    for copy in g_copies:
        copy.wait_recv()
    cut = h_src[r].astype(jnp.float32)
    for k in range(1, GROUPS):
        cut = cut + g_dst[k].astype(jnp.float32)
    h_dst[r] = cut.astype(jnp.bfloat16)
    h_copies = [
        send(h_dst.at[r], h_dst.at[r], h_send.at[k], h_recv.at[k], along_r(k)) for k in range(1, GROUPS)
    ]

    z_w.wait_recv()
    w1_other = w_first(1, 1 - zh)

    for copy in rs_copies_x + rs_copies_y:
        copy.wait_recv()
    rs2 = []
    for k in ORDER:
        acc = p_x[0, k].astype(jnp.float32)
        for j in range(3):
            acc = acc + r_x[j, k].astype(jnp.float32)
        s_x[k - 1] = acc.astype(jnp.bfloat16)
        rs2.append(send(s_x.at[k - 1], q_x.at[k - 1], rs_send.at[1, 0, k - 1], rs_recv.at[1, 0, k - 1], along_y(k)))
        acc = p_y[0, k].astype(jnp.float32)
        for j in range(3):
            acc = acc + r_y[j, k].astype(jnp.float32)
        s_y[k - 1] = acc.astype(jnp.bfloat16)
        rs2.append(send(s_y.at[k - 1], q_y.at[k - 1], rs_send.at[1, 1, k - 1], rs_recv.at[1, 1, k - 1], along_x(k)))

    for copy in w1_own:
        copy.wait_recv()
    w2_own = w_second(0, zh)
    for copy in w1_other:
        copy.wait_recv()
    w2_other = w_second(1, 1 - zh)
    wc = w_core(0, zh, 0) + w_core(1, 1 - zh, 0)

    loads[4].wait()
    loads[5].wait()
    for copy in h_copies:
        copy.wait_recv()
    for j in range(GROUPS):
        g_wide[j * CUT:(j + 1) * CUT, :] = h_dst[j].astype(jnp.float32)[0:CUT]
    average = g_wide[...] / GROUPS
    new_moment = outer_beta * mom_buf[...] + average
    mom_buf[...] = new_moment
    par_buf[...] = par_buf[...] - outer_rate * (average + outer_beta * new_moment)
    stores = [
        pltpu.make_async_copy(par_buf, params_out, store_sem.at[0]),
        pltpu.make_async_copy(mom_buf, moment_out, store_sem.at[1]),
    ]
    for copy in stores:
        copy.start()

    for copy in rs2:
        copy.wait_recv()
    for i, (p, rr, q) in enumerate(((p_x, r_x, q_x), (p_y, r_y, q_y))):
        acc = p[0, 0].astype(jnp.float32)
        for j in range(3):
            acc = acc + rr[j, 0].astype(jnp.float32)
        for j in range(3):
            acc = acc + q[j].astype(jnp.float32)
        total[:, i * PART:(i + 1) * PART] = acc.T
    other = pl.ds(pl.multiple_of((1 - zh) * 2 * ROWS, 16), 2 * ROWS)
    z_src[...] = total[other, :].astype(jnp.bfloat16)
    z_g = send(z_src, z_dst, z_send.at[1], z_recv.at[1], across)

    for s, plane, copies in ((0, zh, w2_own), (1, 1 - zh, w2_other)):
        for i, k in enumerate(ORDER):
            copies[2 * i].wait_recv()
            copies[2 * i + 1].wait_recv()
            wc += w_core(s, plane, k)
    for copy in wc:
        copy.wait_recv()
    own_c = c_buf[0]

    def row(j, _):
        def col(i, _):
            blk = lax.dot_general(
                own_c, w_buf[j, i], (((1,), (1,)), ((), ())), preferred_element_type=jnp.float32
            )
            gi_buf[:, pl.ds(pl.multiple_of((j * 4 + i) * BLOCK, 128), BLOCK)] = blk.astype(jnp.bfloat16)
            return 0

        return lax.fori_loop(0, 4, col, 0)

    lax.fori_loop(0, 4, row, 0)
    gi_store = pltpu.make_async_copy(gi_buf, gi_out, store_sem.at[2])
    gi_store.start()

    z_g.wait_recv()
    first = pl.multiple_of(zh * 2 * ROWS, 16)
    theirs = pl.multiple_of((1 - c) * ROWS, 16)
    ours = pl.multiple_of(c * ROWS, 16)
    swap[...] = total[pl.ds(first + theirs, ROWS), :] + z_dst[pl.ds(theirs, ROWS), :].astype(jnp.float32)
    sw = send(swap, gw_buf.at[:, mine], core_send.at[5], core_recv.at[5], peer)
    gw_buf[:, mine] = total[pl.ds(first + ours, ROWS), :] + z_dst[pl.ds(ours, ROWS), :].astype(jnp.float32)
    sw.wait_recv()
    gw_store = pltpu.make_async_copy(gw_buf, gw_out, store_sem.at[3])
    gw_store.start()

    for copy in sent:
        copy.wait_send()
    for copy in stores:
        copy.wait()
    gi_store.wait()
    gw_store.wait()


def body(activations, up_cotangent, up_weight, pseudo_grads, outer_params, outer_moment):
    bf16, f32 = jnp.bfloat16, jnp.float32
    dma = pltpu.SemaphoreType.DMA
    any_space = pl.BlockSpec(memory_space=pl.ANY)
    gi, gw, new_params, new_moment = pl.pallas_call(
        kernel,
        out_shape=(
            jax.ShapeDtypeStruct((TOK, D), bf16),
            jax.ShapeDtypeStruct((ROWS, FW), f32),
            jax.ShapeDtypeStruct((ROWS, FRAG), f32),
            jax.ShapeDtypeStruct((ROWS, FRAG), f32),
        ),
        in_specs=[any_space] * 6,
        out_specs=(any_space,) * 4,
        scratch_shapes=[
            pltpu.VMEM((2 * TOK, D), bf16),
            pltpu.VMEM((2, TOK, FW), bf16),
            pltpu.VMEM((HALF, 2 * TOK), bf16),
            pltpu.VMEM((4, 4, PART, BLOCK), bf16),
            pltpu.VMEM((4, 4, PART, BLOCK), bf16),
            pltpu.VMEM((3, 4, PART, BLOCK), bf16),
            pltpu.VMEM((3, 4, PART, BLOCK), bf16),
            pltpu.VMEM((3, PART, BLOCK), bf16),
            pltpu.VMEM((3, PART, BLOCK), bf16),
            pltpu.VMEM((3, PART, BLOCK), bf16),
            pltpu.VMEM((3, PART, BLOCK), bf16),
            pltpu.VMEM((BLOCK, HALF), f32),
            pltpu.VMEM((2 * ROWS, HALF), bf16),
            pltpu.VMEM((2 * ROWS, HALF), bf16),
            pltpu.VMEM((ROWS, HALF), f32),
            pltpu.VMEM((ROWS, FW), f32),
            pltpu.VMEM((4, 4, BLOCK, FW), bf16),
            pltpu.VMEM((TOK, D), bf16),
            pltpu.VMEM((ROWS, FRAG), bf16),
            pltpu.VMEM((ROWS, FRAG), f32),
            pltpu.VMEM((GROUPS, PAD, FRAG), f32),
            pltpu.VMEM((GROUPS, PAD, FRAG), bf16),
            pltpu.VMEM((GROUPS, PAD, FRAG), bf16),
            pltpu.VMEM((GROUPS, PAD, FRAG), bf16),
            pltpu.VMEM((ROWS, FRAG), f32),
            pltpu.VMEM((ROWS, FRAG), f32),
            dma((6,)),
            dma((4,)),
            dma((6,)),
            dma((6,)),
            dma((2, 2, 3)),
            dma((2, 2, 3)),
            dma((2,)),
            dma((2,)),
            dma((2, 2, 3)),
            dma((2, 2, 3)),
            dma((2, 2, 3)),
            dma((2, 2, 3)),
            dma((2, 2, 4)),
            dma((2, 2, 4)),
            dma((GROUPS,)),
            dma((GROUPS,)),
            dma((GROUPS,)),
            dma((GROUPS,)),
        ],
        compiler_params=pltpu.CompilerParams(
            collective_id=0, has_side_effects=True, vmem_limit_bytes=62 * 1024 * 1024
        ),
        cost_estimate=pl.CostEstimate(flops=2 * 2 * TOK * D * FW, bytes_accessed=8 << 20, transcendentals=0),
        name="up_backward",
    )(
        activations[0], up_cotangent[0], up_weight[0], pseudo_grads[0], outer_params, outer_moment
    )
    return gi[None], gw[None], new_params, new_moment


def solution(mesh):
    placed = (
        P("replica", "fsdp", None),
        P("replica", "fsdp", None),
        P("replica", "fsdp", None),
        P("replica", "fsdp", None),
        P("fsdp", None),
        P("fsdp", None),
    )
    return jax.shard_map(
        body,
        mesh=mesh,
        in_specs=placed,
        out_specs=(
            P("replica", "fsdp", None),
            P("replica", "fsdp", None),
            P("fsdp", None),
            P("fsdp", None),
        ),
        check_vma=False,
    )
```

time: 394 us -> 81.9 us (0.21)
  waiting for transfers between devices: 336 us -> 0 us
  Pallas kernels: 0 us -> 76.3 us
  starting transfers between devices: 22.5 us -> 0 us
  between operations: 15.5 us -> 0.67 us
  matrix products: 11.6 us -> 0 us
    psum x1 -> x0, waiting for transfers between devices: 180 us -> none  [body(): lax.psum(pseudo_grads[0].astype(jnp.float32).astype(jnp.bfloat16), 'repli...]
    all_gather x2 -> x0, waiting for transfers between devices: 154 us -> none  [the longest x1 153 us: body(): all_cotangent = lax.all_gather(own_cotangent, 'fsdp', axis=0, tiled=True)]
    pallas_call x0 -> x1, Pallas kernels: none -> 76.3 us  [body(): pl.pallas_call(kernel, out_shape=(jax.ShapeDtypeStruct((TOK, D), bf16), j...]
    all_to_all x1 -> x0, starting transfers between devices: 22.4 us -> none  [body(): lax.all_to_all(own_tokens, 'fsdp', split_axis=1, concat_axis=0, tiled=True)]
    dot_general x2 -> x0, matrix products: 11.6 us -> none  [the longest x1 6.08 us: body(): lax.dot_general(own_cotangent, lax.all_gather(own_rows, 'fsdp', axis=0, t...]
  transfers between devices with their start and end apart: 4 -> 0, of which waited for: 3 -> 0; matrix products, arithmetic and copies ran while one was open for 3% -> 0% of each run, Pallas kernels for 0% -> 0%
where the time goes in v1:
time: 81.9 us; the launch traced here: 81.7 us
  Pallas kernels  76.3 us (93%)
  local copies, waits for them, and re-layouts  4.75 us (6%)
    pallas_call x1, Pallas kernels, body(): pl.pallas_call(kernel, out_shape=(jax.ShapeDtypeStruct((TOK, D), bf16), j...  76.3 us
    unnamed x10, local copies, waits for them, and re-layouts  4.75 us

profile of v1, /device:TPU:1, one launch (start us, length us, event | category | flops | bytes accessed | tf_op | source)
XLA Modules:
  0.0 81.7 jit_solution(12639053346716430326)
XLA Ops:
  0.6 76.3 %up_backward.1 = (bf16[128,6144]{1,0:T(8,128)(2,1)}, f32[96,512]{1,0:T(8,128)}, f32[96,384]{1,0:T(8,128)}, f32[96,384]{1,0:T(8,128)}) custom-call(bf16[128,6144]{1,0:T(8,128)(2,1)} %bitcast.8, bf16[128,512]{1,0:T(8,128)(2,1)} %bitcast.9, bf16[96,512]{1,0:T(8,128)(2,1)} %bitcast.10, bf16[96,384]{1,0:T(8,128)(2,1)} %bitcast.11, f32[96,384]{1,0:T(8,128)} %params.1, ...), custom_call_target="tpu_custom_call" | custom-call | flops 1610612736 | bytes 8388608 | tf_op jit(solution)/shard_map/up_backward/pallas_call | solution.py:282
  76.9 0.0 copy-start
  76.9 0.0 copy-start.2
  76.9 0.0 copy-start.1
  76.9 2.7 %copy.14 = bf16[1,128,6144]{2,1,0:T(8,128)(2,1)} copy(bf16[1,128,6144]{2,1,0:T(8,128)(2,1)} %bitcast.6) | data formatting | bytes 3145728
  79.7 0.0 copy-done
  79.7 0.7 copy.15
  80.4 0.0 copy-done.2
  80.4 0.7 copy.16
  81.0 0.0 copy-done.1
  81.0 0.7 copy.17
Async XLA Ops:
  76.9 2.8 %copy-start = (f32[96,512]{1,0:T(8,128)S(1)}, f32[96,512]{1,0:T(8,128)}, u32[]{:S(2)}) copy-start(f32[96,512]{1,0:T(8,128)} %get-tuple-element.9) | copy-start | bytes 589828
  76.9 3.4 %copy-start.2 = (f32[96,384]{1,0:T(8,128)S(1)}, f32[96,384]{1,0:T(8,128)}, u32[]{:S(2)}) copy-start(f32[96,384]{1,0:T(8,128)} %get-tuple-element.18) | copy-start | bytes 442372
  76.9 4.1 %copy-start.1 = (f32[96,384]{1,0:T(8,128)S(1)}, f32[96,384]{1,0:T(8,128)}, u32[]{:S(2)}) copy-start(f32[96,384]{1,0:T(8,128)} %get-tuple-element.19) | copy-start | bytes 442372

commit v2 on v1

v2 whole, which is shorter than its diff:
```python
import functools

import jax
import jax.numpy as jnp
from jax import lax
from jax.experimental import pallas as pl
from jax.experimental.pallas import tpu as pltpu
from jax.sharding import PartitionSpec as P

outer_rate = 0.7
outer_beta = 0.9

SIDE = 4
GROUPS = 8
TOK = 128
ROWS = 96
D = 6144
FW = 512
HALF = FW // 2
PART = HALF // 2
BLOCK = 4 * ROWS
FRAG = 384
CUT = ROWS // GROUPS
PAD = 16
HROWS = ROWS // 2

MESH = pl.DeviceIdType.MESH
ORDER = (1, 3, 2)
A_ORDER = [(j, 2) for j in range(4)] + [(2, k) for k in (0, 1, 3)]
A_ORDER += [(j, k) for j in (1, 3, 0) for k in (0, 1, 3)]


def kernel(
    act, cot, weight, pseudo, params, moment,
    gi_out, gw_out, params_out, moment_out,
    a_buf, c_buf, ct_buf, p_x, p_y, r_x, r_y, s_x, s_y, q_x, q_y, total, z_src, z_dst, swap,
    w_buf, g_buf, g_wide, g_src, g_dst, h_src, h_dst, par_buf, mom_buf,
    load_sem, core_send, core_recv, a_send, a_recv, rs_send, rs_recv, rs2_send, rs2_recv, z_send, z_recv,
    w1_send, w1_recv, w2_send, w2_recv, wc_send, wc_recv, g_send, g_recv, h_send, h_recv,
):
    r = lax.axis_index("replica")
    f = lax.axis_index("fsdp")
    y, x, zh, c = f // 16, (f // 4) % 4, (f // 2) % 2, f % 2

    def at(y, x, zh, c):
        return (r, ((y * 4 + x) * 2 + zh) * 2 + c)

    def along_x(k):
        return at(y, (x + k) % 4, zh, c)

    def along_y(k):
        return at((y + k) % 4, x, zh, c)

    def along_r(k):
        return ((r + k) % GROUPS, f)

    peer = at(y, x, zh, 1 - c)
    across = at(y, x, 1 - zh, c)

    sent = []

    def send(src, dst, ss, rs, to):
        copy = pltpu.make_async_remote_copy(
            src_ref=src, dst_ref=dst, send_sem=ss, recv_sem=rs, device_id=to, device_id_type=MESH
        )
        copy.start()
        sent.append(copy)
        return copy

    own_w = w_buf.at[y, x, pl.ds(pl.multiple_of((zh * 2 + c) * ROWS, ROWS), ROWS)]
    loads = [
        pltpu.make_async_copy(weight, own_w, load_sem.at[0]),
        pltpu.make_async_copy(cot, c_buf.at[0], load_sem.at[1]),
        pltpu.make_async_copy(act, a_buf.at[pl.ds(0, TOK)], load_sem.at[2]),
        pltpu.make_async_copy(pseudo, g_buf, load_sem.at[3]),
        pltpu.make_async_copy(params, par_buf, load_sem.at[4]),
        pltpu.make_async_copy(moment, mom_buf, load_sem.at[5]),
    ]
    for copy in loads:
        copy.start()

    barrier = pltpu.get_barrier_semaphore()
    friends = [peer, across]
    friends += [along_x(k) for k in ORDER] + [along_y(k) for k in ORDER]
    friends += [along_r(k) for k in range(1, GROUPS)]
    for to in friends:
        pl.semaphore_signal(barrier, inc=1, device_id=to, device_id_type=MESH)

    loads[3].wait()
    g_wide[...] = g_buf[...].astype(jnp.float32)
    for j in range(GROUPS):
        g_src[j, 0:CUT, :] = g_wide[j * CUT:(j + 1) * CUT, :]
        g_src[j, CUT:PAD, :] = jnp.zeros((PAD - CUT, FRAG), jnp.float32)
    for j in range(GROUPS):
        h_src[j] = g_src[j].astype(jnp.bfloat16)
    loads[0].wait()
    loads[1].wait()
    loads[2].wait()
    pl.semaphore_wait(barrier, len(friends))

    z_w = send(own_w, own_w, z_send.at[0], z_recv.at[0], across)
    c_copy = send(c_buf.at[0], c_buf.at[1], core_send.at[0], core_recv.at[0], peer)

    def a_cols(j, k):
        return pl.ds(pl.multiple_of((((y + k) % 4) * 4 + (x + j) % 4) * BLOCK, 128), BLOCK)

    def a_one(j, k):
        return pltpu.make_async_remote_copy(
            src_ref=a_buf.at[pl.ds(0, TOK), a_cols(j, k)], dst_ref=a_buf.at[pl.ds(TOK, TOK), a_cols(j, k)],
            send_sem=a_send.at[j, k], recv_sem=a_recv.at[j, k], device_id=peer, device_id_type=MESH,
        )

    for j, k in A_ORDER:
        a_one(j, k).start()

    def w_rows(plane, second):
        return pl.ds(pl.multiple_of((plane * 2 + c) * ROWS + second * HROWS, 16), HROWS)

    def w_first(s, plane):
        copies = []
        for k in ORDER:
            ref = w_buf.at[y, x, w_rows(plane, 0)]
            copies.append(send(ref, ref, w1_send.at[s, 0, k - 1], w1_recv.at[s, 0, k - 1], along_x(k)))
            ref = w_buf.at[y, x, w_rows(plane, 1)]
            copies.append(send(ref, ref, w1_send.at[s, 1, k - 1], w1_recv.at[s, 1, k - 1], along_y(k)))
        return copies

    def w_second(s, plane):
        copies = []
        for d, to in ((0, 1), (1, 3)):
            ref = w_buf.at[y, :, w_rows(plane, 0)]
            copies.append(send(ref, ref, w2_send.at[s, 0, 0, d], w2_recv.at[s, 0, 0, d], along_y(to)))
            ref = w_buf.at[:, x, w_rows(plane, 1)]
            copies.append(send(ref, ref, w2_send.at[s, 1, 0, d], w2_recv.at[s, 1, 0, d], along_x(to)))
        return copies

    def w_third(s, plane, copies):
        out, core = [], []
        for d, to in ((0, 1), (1, 3)):
            copies[2 * d].wait_recv()
            ref = w_buf.at[(y - to) % 4, pl.ds(2 * d, 2), w_rows(plane, 0)]
            out.append(send(ref, ref, w2_send.at[s, 0, 1, d], w2_recv.at[s, 0, 1, d], along_y(to)))
            copies[2 * d + 1].wait_recv()
            ref = w_buf.at[pl.ds(2 * d, 2), (x - to) % 4, w_rows(plane, 1)]
            out.append(send(ref, ref, w2_send.at[s, 1, 1, d], w2_recv.at[s, 1, 1, d], along_x(to)))
            core += w_core(s, plane, to)
        return out, core

    def w_core(s, plane, k):
        ref = w_buf.at[(y - k) % 4, :, w_rows(plane, 0)]
        one = send(ref, ref, wc_send.at[s, 0, k], wc_recv.at[s, 0, k], peer)
        ref = w_buf.at[:, (x - k) % 4, w_rows(plane, 1)]
        two = send(ref, ref, wc_send.at[s, 1, k], wc_recv.at[s, 1, k], peer)
        return [one, two]

    w1_own = w_first(0, zh)

    c_copy.wait_recv()
    mine = pl.ds(pl.multiple_of(c * HALF, HALF), HALF)
    ct_buf[:, 0:TOK] = c_buf[0, :, mine].T
    ct_buf[:, TOK:2 * TOK] = c_buf[1, :, mine].T

    def block(i, _, pick):
        j, k = pick(i)
        a_one(j, k).wait_recv()
        part = jnp.dot(ct_buf[...], a_buf[:, a_cols(j, k)], preferred_element_type=jnp.float32)
        part = part.astype(jnp.bfloat16)
        p_x[j, k] = part[0:PART]
        p_y[k, j] = part[PART:HALF]
        return 0

    def blocks(count, pick):
        lax.fori_loop(0, count, functools.partial(block, pick=pick), 0)

    axes = ((p_x, r_x, s_x, q_x, along_x, along_y), (p_y, r_y, s_y, q_y, along_y, along_x))

    def two_away(axis):
        p, rr, _, _, along, _ = axes[axis]
        return [
            send(p.at[2, pl.ds(2 * d, 2)], rr.at[0, d], rs_send.at[axis, 0, d], rs_recv.at[axis, 0, d], along(to))
            for d, to in ((0, 1), (1, 3))
        ]

    def plain(axis):
        p, rr, _, _, along, _ = axes[axis]
        return [
            send(p.at[to, pl.ds(2 - 2 * d, 2)], rr.at[1, d], rs_send.at[axis, 1, d], rs_recv.at[axis, 1, d], along(to))
            for d, to in ((0, 1), (1, 3))
        ]

    def added(axis, copies):
        p, rr, _, _, along, _ = axes[axis]
        out = []
        for d, to in ((0, 1), (1, 3)):
            copies[d].wait_recv()
            for j in range(2):
                acc = p[to, 2 * d + j].astype(jnp.float32) + rr[0, d, j].astype(jnp.float32)
                p[to, 2 * d + j] = acc.astype(jnp.bfloat16)
            out.append(
                send(p.at[to, pl.ds(2 * d, 2)], rr.at[2, d], rs_send.at[axis, 2, d], rs_recv.at[axis, 2, d], along(to))
            )
        return out

    def gathered(axis, k):
        p, rr = axes[axis][:2]
        left, right = (2, 1) if k < 2 else (1, 2)
        acc = p[0, k].astype(jnp.float32)
        acc = acc + rr[left, 0, k % 2].astype(jnp.float32)
        return acc + rr[right, 1, k % 2].astype(jnp.float32)

    blocks(4, lambda i: (i, 2))
    far_y = two_away(1)
    blocks(3, lambda i: (2, i + i // 2))
    far_x = two_away(0)
    blocks(6, lambda i: (1 + 2 * (i // 3), i % 3 + (i % 3) // 2))
    near_x = plain(0)
    blocks(3, lambda i: (0, i + i // 2))
    near_y = plain(1)

    g_copies = []
    for k in range(1, GROUPS):
        g_copies.append(
            send(h_src.at[(r + k) % GROUPS], g_dst.at[k], g_send.at[k], g_recv.at[k], along_r(k))
        )

    near_y += added(1, far_y)
    near_x += added(0, far_x)

    for copy in g_copies:
        copy.wait_recv()
    cut = h_src[r].astype(jnp.float32)
    for k in range(1, GROUPS):
        cut = cut + g_dst[k].astype(jnp.float32)
    h_dst[r] = cut.astype(jnp.bfloat16)
    h_copies = [
        send(h_dst.at[r], h_dst.at[r], h_send.at[k], h_recv.at[k], along_r(k)) for k in range(1, GROUPS)
    ]

    z_w.wait_recv()
    w1_other = w_first(1, 1 - zh)

    for copy in near_x + near_y:
        copy.wait_recv()
    rs2 = []
    for k in (2, 1, 3):
        for axis in (0, 1):
            _, _, out, landing, _, along = axes[axis]
            out[k - 1] = gathered(axis, k).astype(jnp.bfloat16)
            rs2.append(
                send(out.at[k - 1], landing.at[k - 1], rs2_send.at[axis, k - 1], rs2_recv.at[axis, k - 1], along(k))
            )

    for copy in w1_own:
        copy.wait_recv()
    w2_own = w_second(0, zh)
    for copy in w1_other:
        copy.wait_recv()
    w2_other = w_second(1, 1 - zh)
    wc = w_core(0, zh, 0) + w_core(1, 1 - zh, 0)

    loads[4].wait()
    loads[5].wait()
    for copy in h_copies:
        copy.wait_recv()
    for j in range(GROUPS):
        g_wide[j * CUT:(j + 1) * CUT, :] = h_dst[j].astype(jnp.float32)[0:CUT]
    average = g_wide[...] / GROUPS
    new_moment = outer_beta * mom_buf[...] + average
    moment_out[...] = new_moment
    params_out[...] = par_buf[...] - outer_rate * (average + outer_beta * new_moment)

    for copy in rs2:
        copy.wait_recv()
    for axis in (0, 1):
        acc = gathered(axis, 0)
        for j in range(3):
            acc = acc + axes[axis][3][j].astype(jnp.float32)
        total[:, axis * PART:(axis + 1) * PART] = acc.T
    other = pl.ds(pl.multiple_of((1 - zh) * 2 * ROWS, 16), 2 * ROWS)
    z_src[...] = total[other, :].astype(jnp.bfloat16)
    z_g = send(z_src, z_dst, z_send.at[1], z_recv.at[1], across)

    w3_own, more = w_third(0, zh, w2_own)
    wc += more
    w3_other, more = w_third(1, 1 - zh, w2_other)
    wc += more
    for s, plane, copies in ((0, zh, w3_own), (1, 1 - zh, w3_other)):
        for copy in copies:
            copy.wait_recv()
        wc += w_core(s, plane, 2)
    for copy in wc:
        copy.wait_recv()
    own_c = c_buf[0]

    def row(j, _):
        def col(i, _):
            blk = lax.dot_general(
                own_c, w_buf[j, i], (((1,), (1,)), ((), ())), preferred_element_type=jnp.float32
            )
            gi_out[:, pl.ds(pl.multiple_of((j * 4 + i) * BLOCK, 128), BLOCK)] = blk.astype(jnp.bfloat16)
            return 0

        return lax.fori_loop(0, 4, col, 0)

    lax.fori_loop(0, 4, row, 0)

    z_g.wait_recv()
    first = pl.multiple_of(zh * 2 * ROWS, 16)
    theirs = pl.multiple_of((1 - c) * ROWS, 16)
    ours = pl.multiple_of(c * ROWS, 16)
    swap[...] = total[pl.ds(first + theirs, ROWS), :] + z_dst[pl.ds(theirs, ROWS), :].astype(jnp.float32)
    sw = send(swap, gw_out.at[:, mine], core_send.at[1], core_recv.at[1], peer)
    gw_out[:, mine] = total[pl.ds(first + ours, ROWS), :] + z_dst[pl.ds(ours, ROWS), :].astype(jnp.float32)
    sw.wait_recv()

    for copy in sent:
        copy.wait_send()
    for j, k in A_ORDER:
        a_one(j, k).wait_send()


def store(*refs):
    sems = refs[8]
    copies = [pltpu.make_async_copy(refs[i], refs[4 + i], sems.at[i]) for i in range(4)]
    for copy in copies:
        copy.start()
    for copy in copies:
        copy.wait()


def body(activations, up_cotangent, up_weight, pseudo_grads, outer_params, outer_moment):
    bf16, f32 = jnp.bfloat16, jnp.float32
    dma = pltpu.SemaphoreType.DMA
    any_space = pl.BlockSpec(memory_space=pl.ANY)
    shapes = (((TOK, D), bf16), ((ROWS, FW), f32), ((ROWS, FRAG), f32), ((ROWS, FRAG), f32))
    vmem = pl.BlockSpec(memory_space=pltpu.VMEM)
    results = pl.pallas_call(
        kernel,
        out_shape=tuple(pltpu.VMEM(*shape) for shape in shapes),
        in_specs=[any_space] * 6,
        out_specs=(vmem,) * 4,
        scratch_shapes=[
            pltpu.VMEM((2 * TOK, D), bf16),
            pltpu.VMEM((2, TOK, FW), bf16),
            pltpu.VMEM((HALF, 2 * TOK), bf16),
            pltpu.VMEM((4, 4, PART, BLOCK), bf16),
            pltpu.VMEM((4, 4, PART, BLOCK), bf16),
            pltpu.VMEM((3, 2, 2, PART, BLOCK), bf16),
            pltpu.VMEM((3, 2, 2, PART, BLOCK), bf16),
            pltpu.VMEM((3, PART, BLOCK), bf16),
            pltpu.VMEM((3, PART, BLOCK), bf16),
            pltpu.VMEM((3, PART, BLOCK), bf16),
            pltpu.VMEM((3, PART, BLOCK), bf16),
            pltpu.VMEM((BLOCK, HALF), f32),
            pltpu.VMEM((2 * ROWS, HALF), bf16),
            pltpu.VMEM((2 * ROWS, HALF), bf16),
            pltpu.VMEM((ROWS, HALF), f32),
            pltpu.VMEM((4, 4, BLOCK, FW), bf16),
            pltpu.VMEM((ROWS, FRAG), bf16),
            pltpu.VMEM((ROWS, FRAG), f32),
            pltpu.VMEM((GROUPS, PAD, FRAG), f32),
            pltpu.VMEM((GROUPS, PAD, FRAG), bf16),
            pltpu.VMEM((GROUPS, PAD, FRAG), bf16),
            pltpu.VMEM((GROUPS, PAD, FRAG), bf16),
            pltpu.VMEM((ROWS, FRAG), f32),
            pltpu.VMEM((ROWS, FRAG), f32),
            dma((6,)),
            dma((2,)),
            dma((2,)),
            dma((4, 4)),
            dma((4, 4)),
            dma((2, 3, 2)),
            dma((2, 3, 2)),
            dma((2, 3)),
            dma((2, 3)),
            dma((2,)),
            dma((2,)),
            dma((2, 2, 3)),
            dma((2, 2, 3)),
            dma((2, 2, 2, 2)),
            dma((2, 2, 2, 2)),
            dma((2, 2, 4)),
            dma((2, 2, 4)),
            dma((GROUPS,)),
            dma((GROUPS,)),
            dma((GROUPS,)),
            dma((GROUPS,)),
        ],
        compiler_params=pltpu.CompilerParams(
            collective_id=0, has_side_effects=True, vmem_limit_bytes=61 * 1024 * 1024
        ),
        cost_estimate=pl.CostEstimate(flops=2 * 2 * TOK * D * FW, bytes_accessed=8 << 20, transcendentals=0),
        name="up_backward",
    )(
        activations[0], up_cotangent[0], up_weight[0], pseudo_grads[0], outer_params, outer_moment
    )
    gi, gw, new_params, new_moment = pl.pallas_call(
        store,
        out_shape=tuple(jax.ShapeDtypeStruct(*shape) for shape in shapes),
        in_specs=[vmem] * 4,
        out_specs=(any_space,) * 4,
        scratch_shapes=[dma((4,))],
        name="store_results",
    )(*results)
    return gi[None], gw[None], new_params, new_moment


def solution(mesh):
    placed = (
        P("replica", "fsdp", None),
        P("replica", "fsdp", None),
        P("replica", "fsdp", None),
        P("replica", "fsdp", None),
        P("fsdp", None),
        P("fsdp", None),
    )
    return jax.shard_map(
        body,
        mesh=mesh,
        in_specs=placed,
        out_specs=(
            P("replica", "fsdp", None),
            P("replica", "fsdp", None),
            P("fsdp", None),
            P("fsdp", None),
        ),
        check_vma=False,
    )
```

time: 81.9 us -> 71.9 us (0.88)
  Pallas kernels: 76.3 us -> 67.9 us
  local copies, waits for them, and re-layouts: 4.75 us -> 3.15 us
    pallas_call x1 -> x2, Pallas kernels: 76.3 us -> 67.9 us  [the longest x1 65 us: body(): pl.pallas_call(kernel, out_shape=tuple((pltpu.VMEM(*shape) for shape in s...]
    unnamed x10 -> x8, local copies, waits for them, and re-layouts: 4.75 us -> 3.15 us
where the time goes in v2:
time: 71.9 us; the launch traced here: 71.7 us
  Pallas kernels  67.9 us (94%)
  local copies, waits for them, and re-layouts  3.15 us (4%)
    pallas_call x1, Pallas kernels, body(): pl.pallas_call(kernel, out_shape=tuple((pltpu.VMEM(*shape) for shape in s...  65 us
    unnamed x8, local copies, waits for them, and re-layouts  3.15 us
    pallas_call x1, Pallas kernels, body(): pl.pallas_call(store, out_shape=tuple((jax.ShapeDtypeStruct(*shape) for s...  2.85 us

profile of v2, /device:TPU:1, one launch (start us, length us, event | category | flops | bytes accessed | tf_op | source)
XLA Modules:
  0.0 71.7 jit_solution(18235748296847153356)
XLA Ops:
  0.6 65.0 %up_backward.1 = (bf16[128,6144]{1,0:T(8,128)(2,1)S(1)}, f32[96,512]{1,0:T(8,128)S(1)}, f32[96,384]{1,0:T(8,128)S(1)}, f32[96,384]{1,0:T(8,128)S(1)}) custom-call(bf16[128,6144]{1,0:T(8,128)(2,1)} %bitcast.6, bf16[128,512]{1,0:T(8,128)(2,1)} %bitcast.9, bf16[96,512]{1,0:T(8,128)(2,1)} %bitcast.10, bf16[96,384]{1,0:T(8,128)(2,1)} %bitcast.11, ...), custom_call_target="tpu_custom_call" | custom-call | flops 1610612736 | bytes 8388608 | tf_op jit(solution)/shard_map/up_backward/pallas_call | solution.py:337
  65.7 0.0 copy-start
  65.7 1.1 %copy-done = bf16[128,6144]{1,0:T(8,128)(2,1)} copy-done((bf16[128,6144]{1,0:T(8,128)(2,1)}, bf16[128,6144]{1,0:T(8,128)(2,1)S(1)}, u32[]{:S(2)}) %copy-start) | copy-done | bytes 1572888
  66.8 0.0 copy-start.1
  66.8 0.7 copy-done.1
  67.5 0.0 copy-start.2
  67.5 0.7 copy-done.2
  68.2 0.0 copy-start.3
  68.2 0.7 copy-done.3
  68.8 2.9 %store_results.1 = (bf16[128,6144]{1,0:T(8,128)(2,1)}, f32[96,512]{1,0:T(8,128)}, f32[96,384]{1,0:T(8,128)}, f32[96,384]{1,0:T(8,128)}) custom-call(bf16[128,6144]{1,0:T(8,128)(2,1)} %copy-done, f32[96,512]{1,0:T(8,128)} %copy-done.1, f32[96,384]{1,0:T(8,128)} %copy-done.2, f32[96,384]{1,0:T(8,128)} %copy-done.3), custom_call_target="tpu_custom_call" | custom-call | tf_op jit(solution)/shard_map/store_results/pallas_call | solution.py:397
Async XLA Ops:
  65.7 1.2 %copy-start = (bf16[128,6144]{1,0:T(8,128)(2,1)}, bf16[128,6144]{1,0:T(8,128)(2,1)S(1)}, u32[]{:S(2)}) copy-start(bf16[128,6144]{1,0:T(8,128)(2,1)S(1)} %get-tuple-element.12.refs_0_) | copy-start | bytes 4718596
  66.8 0.7 copy-start.1
  67.5 0.7 copy-start.2
  68.2 0.7 copy-start.3

commit v3 on v2

v3 whole, which is shorter than its diff:
```python
import jax
import jax.numpy as jnp
from jax import lax
from jax.experimental import pallas as pl
from jax.experimental.pallas import tpu as pltpu
from jax.sharding import PartitionSpec as P

outer_rate = 0.7
outer_beta = 0.9

SIDE = 4
GROUPS = 8
TOK = 128
ROWS = 96
D = 6144
FW = 512
HALF = FW // 2
PART = HALF // 2
BLOCK = 4 * ROWS
FRAG = 384
CUT = ROWS // GROUPS
PAD = 16
HROWS = ROWS // 2

MESH = pl.DeviceIdType.MESH
ORDER = (1, 3, 2)
TWO_AWAY = ((2, 2), (0, 2), (2, 0), (1, 2), (2, 1), (3, 2), (2, 3))
PLAIN = ((1, 3), (3, 1), (3, 0), (0, 3))
REST = ((1, 0), (1, 1), (3, 3), (0, 1), (0, 0))
A_ORDER = TWO_AWAY + PLAIN + REST
PIECE = PART // 2


def kernel(
    act, cot, weight, pseudo, params, moment,
    gi_out, gw_out, params_out, moment_out,
    a_buf, c_buf, ct_buf, p_x, p_y, r_x, r_y, s_x, s_y, q_x, q_y, total, z_src, z_dst, swapped, gw_buf,
    w_buf, gi_buf, g_buf, g_wide, g_src, g_dst, h_src, h_dst, par_buf, mom_buf,
    load_sem, store_sem, core_send, core_recv, a_send, a_recv, rs_send, rs_recv, rs2_send, rs2_recv, z_send, z_recv,
    w1_send, w1_recv, w2_send, w2_recv, wc_send, wc_recv, g_send, g_recv, h_send, h_recv,
):
    r = lax.axis_index("replica")
    f = lax.axis_index("fsdp")
    y, x, zh, c = f // 16, (f // 4) % 4, (f // 2) % 2, f % 2

    def at(y, x, zh, c):
        return (r, ((y * 4 + x) * 2 + zh) * 2 + c)

    def along_x(k):
        return at(y, (x + k) % 4, zh, c)

    def along_y(k):
        return at((y + k) % 4, x, zh, c)

    def along_r(k):
        return ((r + k) % GROUPS, f)

    peer = at(y, x, zh, 1 - c)
    across = at(y, x, 1 - zh, c)

    sent = []

    def send(src, dst, ss, rs, to):
        copy = pltpu.make_async_remote_copy(
            src_ref=src, dst_ref=dst, send_sem=ss, recv_sem=rs, device_id=to, device_id_type=MESH
        )
        copy.start()
        sent.append(copy)
        return copy

    own_w = w_buf.at[y, x, pl.ds(pl.multiple_of((zh * 2 + c) * ROWS, ROWS), ROWS)]
    loads = [
        pltpu.make_async_copy(weight, own_w, load_sem.at[0]),
        pltpu.make_async_copy(cot, c_buf.at[0], load_sem.at[1]),
        pltpu.make_async_copy(act, a_buf.at[pl.ds(0, TOK)], load_sem.at[2]),
        pltpu.make_async_copy(pseudo, g_buf, load_sem.at[3]),
        pltpu.make_async_copy(params, par_buf, load_sem.at[4]),
        pltpu.make_async_copy(moment, mom_buf, load_sem.at[5]),
    ]
    for copy in loads:
        copy.start()

    barrier = pltpu.get_barrier_semaphore()
    friends = [peer, across, at(y, x, 1 - zh, 1 - c)]
    friends += [along_x(k) for k in ORDER] + [along_y(k) for k in ORDER]
    friends += [along_r(k) for k in range(1, GROUPS)]
    for to in friends:
        pl.semaphore_signal(barrier, inc=1, device_id=to, device_id_type=MESH)

    loads[3].wait()
    g_wide[...] = g_buf[...].astype(jnp.float32)
    for j in range(GROUPS):
        g_src[j, 0:CUT, :] = g_wide[j * CUT:(j + 1) * CUT, :]
        g_src[j, CUT:PAD, :] = jnp.zeros((PAD - CUT, FRAG), jnp.float32)
    for j in range(GROUPS):
        h_src[j] = g_src[j].astype(jnp.bfloat16)
    loads[0].wait()
    loads[1].wait()
    loads[2].wait()
    pl.semaphore_wait(barrier, len(friends))

    z_w = []
    for i in range(2):
        ref = w_buf.at[y, x, pl.ds(pl.multiple_of((zh * 2 + c) * ROWS + i * HROWS, 16), HROWS)]
        z_w.append(send(ref, ref, z_send.at[2 + i], z_recv.at[2 + i], across))
    c_copy = send(c_buf.at[0], c_buf.at[1], core_send.at[0], core_recv.at[0], peer)

    def a_cols(j, k):
        return pl.ds(pl.multiple_of((((y + k) % 4) * 4 + (x + j) % 4) * BLOCK, 128), BLOCK)

    def a_one(j, k):
        return pltpu.make_async_remote_copy(
            src_ref=a_buf.at[pl.ds(0, TOK), a_cols(j, k)], dst_ref=a_buf.at[pl.ds(TOK, TOK), a_cols(j, k)],
            send_sem=a_send.at[j, k], recv_sem=a_recv.at[j, k], device_id=peer, device_id_type=MESH,
        )

    for j, k in A_ORDER:
        a_one(j, k).start()

    def w_rows(plane, second):
        return pl.ds(pl.multiple_of((plane * 2 + c) * ROWS + second * HROWS, 16), HROWS)

    def w_first(s, plane):
        copies = []
        for k in ORDER:
            ref = w_buf.at[y, x, w_rows(plane, 0)]
            copies.append(send(ref, ref, w1_send.at[s, 0, k - 1], w1_recv.at[s, 0, k - 1], along_x(k)))
            ref = w_buf.at[y, x, w_rows(plane, 1)]
            copies.append(send(ref, ref, w1_send.at[s, 1, k - 1], w1_recv.at[s, 1, k - 1], along_y(k)))
        return copies

    def w_second(s, plane, pieces):
        copies = {}
        for i in pieces:
            for d, to in ((0, 1), (1, 3)):
                ref = w_buf.at[y, (x + i) % 4, w_rows(plane, 0)]
                copies[0, d, i] = send(
                    ref, ref, w2_send.at[s, 0, 0, d, i], w2_recv.at[s, 0, 0, d, i], along_y(to)
                )
                ref = w_buf.at[(y + i) % 4, x, w_rows(plane, 1)]
                copies[1, d, i] = send(
                    ref, ref, w2_send.at[s, 1, 0, d, i], w2_recv.at[s, 1, 0, d, i], along_x(to)
                )
        return copies

    def w_third(s, plane, copies):
        out, core = [], []
        for i in range(4):
            d, to = ((0, 1), (1, 3))[i // 2]
            copies[0, d, i].wait_recv()
            ref = w_buf.at[(y - to) % 4, (x + i) % 4, w_rows(plane, 0)]
            out.append(send(ref, ref, w2_send.at[s, 0, 1, d, i], w2_recv.at[s, 0, 1, d, i], along_y(to)))
            copies[1, d, i].wait_recv()
            ref = w_buf.at[(y + i) % 4, (x - to) % 4, w_rows(plane, 1)]
            out.append(send(ref, ref, w2_send.at[s, 1, 1, d, i], w2_recv.at[s, 1, 1, d, i], along_x(to)))
        for i in range(4):
            copies[0, 1 - i // 2, i].wait_recv()
            copies[1, 1 - i // 2, i].wait_recv()
        for k in (1, 3):
            core += w_core(s, plane, k)
        return out, core

    def w_core(s, plane, k):
        ref = w_buf.at[(y - k) % 4, :, w_rows(plane, 0)]
        one = send(ref, ref, wc_send.at[s, 0, k], wc_recv.at[s, 0, k], peer)
        ref = w_buf.at[:, (x - k) % 4, w_rows(plane, 1)]
        two = send(ref, ref, wc_send.at[s, 1, k], wc_recv.at[s, 1, k], peer)
        return [one, two]

    w1_own = w_first(0, zh)
    w2_own = w_second(0, zh, (0,))

    c_copy.wait_recv()
    mine = pl.ds(pl.multiple_of(c * HALF, HALF), HALF)
    ct_buf[:, 0:TOK] = c_buf[0, :, mine].T
    ct_buf[:, TOK:2 * TOK] = c_buf[1, :, mine].T

    axes = ((p_x, r_x, s_x, q_x, along_x, along_y), (p_y, r_y, s_y, q_y, along_y, along_x))
    half = (pl.ds(0, PIECE), pl.ds(PIECE, PIECE))
    rs = {}

    def leave(axis, step, d, j, h):
        p, rr, _, _, along, _ = axes[axis]
        to = (1, 3)[d]
        near = 2 if step == 0 else to
        k = 2 * d + j if step != 1 else 2 - 2 * d + j
        rs[axis, step, d, j, h] = send(
            p.at[near, k, half[h]], rr.at[step, d, j, half[h]],
            rs_send.at[axis, step, d, 2 * j + h], rs_recv.at[axis, step, d, 2 * j + h], along(to),
        )

    def block(j, k):
        a_one(j, k).wait_recv()
        part = jnp.dot(ct_buf[...], a_buf[:, a_cols(j, k)], preferred_element_type=jnp.float32)
        part = part.astype(jnp.bfloat16)
        p_x[j, k] = part[0:PART]
        p_y[k, j] = part[PART:HALF]

    def leave_block(axis, near, far):
        for h in range(2):
            if near == 2:
                leave(axis, 0, far // 2, far % 2, h)
            elif near == 1 and far >= 2:
                leave(axis, 1, 0, far % 2, h)
            elif near == 3 and far < 2:
                leave(axis, 1, 1, far % 2, h)

    def gathered(axis, k):
        p, rr = axes[axis][:2]
        left, right = (2, 1) if k < 2 else (1, 2)
        acc = p[0, k].astype(jnp.float32)
        acc = acc + rr[left, 0, k % 2].astype(jnp.float32)
        return acc + rr[right, 1, k % 2].astype(jnp.float32)

    def arrived(axis, k):
        left, right = (2, 1) if k < 2 else (1, 2)
        for h in range(2):
            rs[axis, left, 0, k % 2, h].wait_recv()
            rs[axis, right, 1, k % 2, h].wait_recv()

    for j, k in TWO_AWAY:
        block(j, k)
        if k == 2:
            leave_block(1, 2, j)
        if j == 2:
            leave_block(0, 2, k)
    for j, k in ((1, 2), (3, 2), (2, 1), (2, 3)) + PLAIN:
        if (j, k) in PLAIN:
            block(j, k)
        if j != 2:
            leave_block(0, j, k)
        if k != 2:
            leave_block(1, k, j)
    for j, k in REST:
        block(j, k)

    g_copies = []
    for k in range(1, GROUPS):
        g_copies.append(
            send(h_src.at[(r + k) % GROUPS], g_dst.at[k], g_send.at[k], g_recv.at[k], along_r(k))
        )

    for d, j in ((1, 0), (0, 0), (0, 1), (1, 1)):
        for h in range(2):
            for axis in (1, 0):
                p, rr = axes[axis][:2]
                rs[axis, 0, d, j, h].wait_recv()
                to = (1, 3)[d]
                acc = p[to, 2 * d + j, half[h], :].astype(jnp.float32) + rr[0, d, j, half[h], :].astype(jnp.float32)
                p[to, 2 * d + j, half[h], :] = acc.astype(jnp.bfloat16)
                leave(axis, 2, d, j, h)

    for copy in w1_own:
        copy.wait_recv()
    w2_own.update(w_second(0, zh, (1, 2, 3)))
    wc = w_core(0, zh, 0)

    rs2 = []
    for k in (2, 1, 3):
        for axis in (1, 0):
            _, _, out, landing, _, along = axes[axis]
            arrived(axis, k)
            out[k - 1] = gathered(axis, k).astype(jnp.bfloat16)
            for h in range(2):
                rs2.append(
                    send(
                        out.at[k - 1, half[h]], landing.at[k - 1, half[h]],
                        rs2_send.at[axis, k - 1, h], rs2_recv.at[axis, k - 1, h], along(k),
                    )
                )

    for copy in g_copies:
        copy.wait_recv()
    cut = h_src[r].astype(jnp.float32)
    for k in range(1, GROUPS):
        cut = cut + g_dst[k].astype(jnp.float32)
    h_dst[r] = cut.astype(jnp.bfloat16)
    h_copies = [
        send(h_dst.at[r], h_dst.at[r], h_send.at[k], h_recv.at[k], along_r(k)) for k in range(1, GROUPS)
    ]

    for copy in z_w:
        copy.wait_recv()
    w1_other = w_first(1, 1 - zh)
    w2_other = w_second(1, 1 - zh, (0,))
    w3_own, more = w_third(0, zh, w2_own)
    wc += more

    for copy in rs2:
        copy.wait_recv()
    for axis in (0, 1):
        arrived(axis, 0)
        acc = gathered(axis, 0)
        for j in range(3):
            acc = acc + axes[axis][3][j].astype(jnp.float32)
        total[:, axis * PART:(axis + 1) * PART] = acc.T

    def rows(plane, core):
        return pl.ds(pl.multiple_of((plane * 2 + core) * ROWS, 16), ROWS)

    z_g = []
    for i, core in enumerate((c, 1 - c)):
        z_src[i] = total[rows(1 - zh, core), :].astype(jnp.bfloat16)
        z_g.append(
            send(z_src.at[i], z_dst.at[i], z_send.at[i], z_recv.at[i], at(y, x, 1 - zh, core))
        )
    swap = send(total.at[rows(zh, 1 - c)], swapped, core_send.at[1], core_recv.at[1], peer)

    for copy in w1_other:
        copy.wait_recv()
    w2_other.update(w_second(1, 1 - zh, (1, 2, 3)))
    wc += w_core(1, 1 - zh, 0)
    for copy in w3_own:
        copy.wait_recv()
    w_last = w_core(0, zh, 2)

    loads[4].wait()
    loads[5].wait()
    for copy in h_copies:
        copy.wait_recv()
    for j in range(GROUPS):
        g_wide[j * CUT:(j + 1) * CUT, :] = h_dst[j].astype(jnp.float32)[0:CUT]
    average = g_wide[...] / GROUPS
    new_moment = outer_beta * mom_buf[...] + average
    mom_buf[...] = new_moment
    par_buf[...] = par_buf[...] - outer_rate * (average + outer_beta * new_moment)
    stores = [
        pltpu.make_async_copy(par_buf, params_out, store_sem.at[0]),
        pltpu.make_async_copy(mom_buf, moment_out, store_sem.at[1]),
    ]
    for copy in stores:
        copy.start()

    w3_other, more = w_third(1, 1 - zh, w2_other)
    wc += more
    own_c = c_buf[0]

    def gi_block(j, k):
        blk = lax.dot_general(
            own_c, w_buf[(y + k) % 4, (x + j) % 4], (((1,), (1,)), ((), ())), preferred_element_type=jnp.float32
        )
        gi_buf[:, a_cols(j, k)] = blk.astype(jnp.bfloat16)

    for copy in wc:
        copy.wait_recv()
    for k in (0, 1, 3):
        for j in (0, 1, 3):
            gi_block(j, k)
    for copy in w3_other:
        copy.wait_recv()
    w_last += w_core(1, 1 - zh, 2)
    for copy in w_last:
        copy.wait_recv()
    for j in range(4):
        gi_block(j, 2)
    for k in (0, 1, 3):
        gi_block(2, k)
    stores.append(pltpu.make_async_copy(gi_buf, gi_out, store_sem.at[2]))
    stores[2].start()

    swap.wait_recv()
    for copy in z_g:
        copy.wait_recv()
    gw_buf[:, mine] = total[rows(zh, c), :] + z_dst[0].astype(jnp.float32)
    others = pl.ds(pl.multiple_of((1 - c) * HALF, HALF), HALF)
    gw_buf[:, others] = swapped[...] + z_dst[1].astype(jnp.float32)
    stores.append(pltpu.make_async_copy(gw_buf, gw_out, store_sem.at[3]))
    stores[3].start()

    for copy in sent:
        copy.wait_send()
    for j, k in A_ORDER:
        a_one(j, k).wait_send()
    for copy in stores:
        copy.wait()


def store(gi, gw, params, moment, gi_out, gw_out, params_out, moment_out, gi_buf, gw_buf, par_buf, mom_buf, sem):
    pieces = [
        (ref.at[pl.ds(i * 32, 32)], buf.at[pl.ds(i * 32, 32)], out.at[pl.ds(i * 32, 32)])
        for ref, buf, out in ((gi, gi_buf, gi_out),)
        for i in range(TOK // 32)
    ]
    pieces += [(gw, gw_buf, gw_out), (params, par_buf, params_out), (moment, mom_buf, moment_out)]
    loads = [pltpu.make_async_copy(p[0], p[1], sem.at[0, i]) for i, p in enumerate(pieces)]
    stores = [pltpu.make_async_copy(p[1], p[2], sem.at[1, i]) for i, p in enumerate(pieces)]
    for copy in loads:
        copy.start()
    for i in range(len(pieces)):
        loads[i].wait()
        stores[i].start()
    for copy in stores:
        copy.wait()


def body(activations, up_cotangent, up_weight, pseudo_grads, outer_params, outer_moment):
    bf16, f32 = jnp.bfloat16, jnp.float32
    dma = pltpu.SemaphoreType.DMA
    any_space = pl.BlockSpec(memory_space=pl.ANY)
    shapes = (((TOK, D), bf16), ((ROWS, FW), f32), ((ROWS, FRAG), f32), ((ROWS, FRAG), f32))
    results = pl.pallas_call(
        kernel,
        out_shape=tuple(jax.ShapeDtypeStruct(*shape) for shape in shapes),
        in_specs=[any_space] * 6,
        out_specs=(any_space,) * 4,
        scratch_shapes=[
            pltpu.VMEM((2 * TOK, D), bf16),
            pltpu.VMEM((2, TOK, FW), bf16),
            pltpu.VMEM((HALF, 2 * TOK), bf16),
            pltpu.VMEM((4, 4, PART, BLOCK), bf16),
            pltpu.VMEM((4, 4, PART, BLOCK), bf16),
            pltpu.VMEM((3, 2, 2, PART, BLOCK), bf16),
            pltpu.VMEM((3, 2, 2, PART, BLOCK), bf16),
            pltpu.VMEM((3, PART, BLOCK), bf16),
            pltpu.VMEM((3, PART, BLOCK), bf16),
            pltpu.VMEM((3, PART, BLOCK), bf16),
            pltpu.VMEM((3, PART, BLOCK), bf16),
            pltpu.VMEM((BLOCK, HALF), f32),
            pltpu.VMEM((2, ROWS, HALF), bf16),
            pltpu.VMEM((2, ROWS, HALF), bf16),
            pltpu.VMEM((ROWS, HALF), f32),
            pltpu.VMEM((ROWS, FW), f32),
            pltpu.VMEM((4, 4, BLOCK, FW), bf16),
            pltpu.VMEM((TOK, D), bf16),
            pltpu.VMEM((ROWS, FRAG), bf16),
            pltpu.VMEM((ROWS, FRAG), f32),
            pltpu.VMEM((GROUPS, PAD, FRAG), f32),
            pltpu.VMEM((GROUPS, PAD, FRAG), bf16),
            pltpu.VMEM((GROUPS, PAD, FRAG), bf16),
            pltpu.VMEM((GROUPS, PAD, FRAG), bf16),
            pltpu.VMEM((ROWS, FRAG), f32),
            pltpu.VMEM((ROWS, FRAG), f32),
            dma((6,)),
            dma((4,)),
            dma((2,)),
            dma((2,)),
            dma((4, 4)),
            dma((4, 4)),
            dma((2, 3, 2, 4)),
            dma((2, 3, 2, 4)),
            dma((2, 3, 2)),
            dma((2, 3, 2)),
            dma((4,)),
            dma((4,)),
            dma((2, 2, 3)),
            dma((2, 2, 3)),
            dma((2, 2, 2, 2, 4)),
            dma((2, 2, 2, 2, 4)),
            dma((2, 2, 4)),
            dma((2, 2, 4)),
            dma((GROUPS,)),
            dma((GROUPS,)),
            dma((GROUPS,)),
            dma((GROUPS,)),
        ],
        compiler_params=pltpu.CompilerParams(
            collective_id=0, has_side_effects=True, vmem_limit_bytes=62 * 1024 * 1024
        ),
        cost_estimate=pl.CostEstimate(flops=2 * 2 * TOK * D * FW, bytes_accessed=8 << 20, transcendentals=0),
        name="up_backward",
    )(
        activations[0], up_cotangent[0], up_weight[0], pseudo_grads[0], outer_params, outer_moment
    )
    gi, gw, new_params, new_moment = pl.pallas_call(
        store,
        out_shape=tuple(jax.ShapeDtypeStruct(*shape) for shape in shapes),
        in_specs=[any_space] * 4,
        out_specs=(any_space,) * 4,
        scratch_shapes=[pltpu.VMEM(*shape) for shape in shapes] + [dma((2, TOK // 32 + 3))],
        compiler_params=pltpu.CompilerParams(vmem_limit_bytes=62 * 1024 * 1024),
        name="store_results",
    )(*results)
    return gi[None], gw[None], new_params, new_moment


def solution(mesh):
    placed = (
        P("replica", "fsdp", None),
        P("replica", "fsdp", None),
        P("replica", "fsdp", None),
        P("replica", "fsdp", None),
        P("fsdp", None),
        P("fsdp", None),
    )
    return jax.shard_map(
        body,
        mesh=mesh,
        in_specs=placed,
        out_specs=(
            P("replica", "fsdp", None),
            P("replica", "fsdp", None),
            P("fsdp", None),
            P("fsdp", None),
        ),
        check_vma=False,
    )
```

time: 71.9 us -> 65 us (0.904)
  Pallas kernels: 67.9 us -> 64.2 us
  local copies, waits for them, and re-layouts: 3.15 us -> 0 us
    pallas_call x1, Pallas kernels: 65 us -> 61.8 us  [body(): pl.pallas_call(kernel, out_shape=tuple((jax.ShapeDtypeStruct(*shape) for...]
    unnamed x8 -> x0, local copies, waits for them, and re-layouts: 3.15 us -> none
where the time goes in v3:
time: 65 us; the launch traced here: 64.9 us
  Pallas kernels  64.2 us (99%)
    pallas_call x1, Pallas kernels, body(): pl.pallas_call(kernel, out_shape=tuple((jax.ShapeDtypeStruct(*shape) for...  61.8 us
    pallas_call x1, Pallas kernels, body(): pl.pallas_call(store, out_shape=tuple((jax.ShapeDtypeStruct(*shape) for s...  2.41 us

profile of v3, /device:TPU:1, one launch (start us, length us, event | category | flops | bytes accessed | tf_op | source)
XLA Modules:
  0.0 64.9 jit_solution(16932531138392740678)
XLA Ops:
  0.6 61.8 %up_backward.1 = (bf16[128,6144]{1,0:T(8,128)(2,1)}, f32[96,512]{1,0:T(8,128)}, f32[96,384]{1,0:T(8,128)}, f32[96,384]{1,0:T(8,128)}) custom-call(bf16[128,6144]{1,0:T(8,128)(2,1)} %bitcast.6, bf16[128,512]{1,0:T(8,128)(2,1)} %bitcast.9, bf16[96,512]{1,0:T(8,128)(2,1)} %bitcast.10, bf16[96,384]{1,0:T(8,128)(2,1)} %bitcast.11, f32[96,384]{1,0:T(8,128)} %params.1, ...), custom_call_target="tpu_custom_call" | custom-call | flops 1610612736 | bytes 8388608 | tf_op jit(solution)/shard_map/up_backward/pallas_call | solution.py:401
  62.5 2.4 %store_results.1 = (bf16[128,6144]{1,0:T(8,128)(2,1)}, f32[96,512]{1,0:T(8,128)}, f32[96,384]{1,0:T(8,128)}, f32[96,384]{1,0:T(8,128)}) custom-call(bf16[128,6144]{1,0:T(8,128)(2,1)} %get-tuple-element.12.gi, f32[96,512]{1,0:T(8,128)} %get-tuple-element.13.gw, f32[96,384]{1,0:T(8,128)} %get-tuple-element.14.params, f32[96,384]{1,0:T(8,128)} %get-tuple-element.15.moment), custom_call_target="tpu_custom_call" | custom-call | tf_op jit(solution)/shard_map/store_results/pallas_call | solution.py:464

commit v4 on v3

--- a/solution.py
+++ b/solution.py
@@ -250,10 +250,10 @@
                 p[to, 2 * d + j, half[h], :] = acc.astype(jnp.bfloat16)
                 leave(axis, 2, d, j, h)
 
-    for copy in w1_own:
-        copy.wait_recv()
-    w2_own.update(w_second(0, zh, (1, 2, 3)))
-    wc = w_core(0, zh, 0)
+    for copy in z_w:
+        copy.wait_recv()
+    w1_other = w_first(1, 1 - zh)
+    w2_other = w_second(1, 1 - zh, (0,))
 
     rs2 = []
     for k in (2, 1, 3):
@@ -269,6 +269,15 @@
                     )
                 )
 
+    for copy in w1_own:
+        copy.wait_recv()
+    w2_own.update(w_second(0, zh, (1, 2, 3)))
+    wc = w_core(0, zh, 0)
+    for copy in w1_other:
+        copy.wait_recv()
+    w2_other.update(w_second(1, 1 - zh, (1, 2, 3)))
+    wc += w_core(1, 1 - zh, 0)
+
     for copy in g_copies:
         copy.wait_recv()
     cut = h_src[r].astype(jnp.float32)
@@ -279,13 +288,6 @@
         send(h_dst.at[r], h_dst.at[r], h_send.at[k], h_recv.at[k], along_r(k)) for k in range(1, GROUPS)
     ]
 
-    for copy in z_w:
-        copy.wait_recv()
-    w1_other = w_first(1, 1 - zh)
-    w2_other = w_second(1, 1 - zh, (0,))
-    w3_own, more = w_third(0, zh, w2_own)
-    wc += more
-
     for copy in rs2:
         copy.wait_recv()
     for axis in (0, 1):
@@ -306,13 +308,10 @@
         )
     swap = send(total.at[rows(zh, 1 - c)], swapped, core_send.at[1], core_recv.at[1], peer)
 
-    for copy in w1_other:
-        copy.wait_recv()
-    w2_other.update(w_second(1, 1 - zh, (1, 2, 3)))
-    wc += w_core(1, 1 - zh, 0)
-    for copy in w3_own:
-        copy.wait_recv()
-    w_last = w_core(0, zh, 2)
+    w3_own, more = w_third(0, zh, w2_own)
+    wc += more
+    w3_other, more = w_third(1, 1 - zh, w2_other)
+    wc += more
 
     loads[4].wait()
     loads[5].wait()
@@ -331,8 +330,9 @@
     for copy in stores:
         copy.start()
 
-    w3_other, more = w_third(1, 1 - zh, w2_other)
-    wc += more
+    for copy in w3_own:
+        copy.wait_recv()
+    w_last = w_core(0, zh, 2)
     own_c = c_buf[0]
 
     def gi_block(j, k):
@@ -340,6 +340,11 @@
             own_c, w_buf[(y + k) % 4, (x + j) % 4], (((1,), (1,)), ((), ())), preferred_element_type=jnp.float32
         )
         gi_buf[:, a_cols(j, k)] = blk.astype(jnp.bfloat16)
+        copy = pltpu.make_async_copy(
+            gi_buf.at[:, a_cols(j, k)], gi_out.at[:, a_cols(j, k)], store_sem.at[3 + 4 * j + k]
+        )
+        copy.start()
+        stores.append(copy)
 
     for copy in wc:
         copy.wait_recv()
@@ -355,8 +360,6 @@
         gi_block(j, 2)
     for k in (0, 1, 3):
         gi_block(2, k)
-    stores.append(pltpu.make_async_copy(gi_buf, gi_out, store_sem.at[2]))
-    stores[2].start()
 
     swap.wait_recv()
     for copy in z_g:
@@ -364,8 +367,8 @@
     gw_buf[:, mine] = total[rows(zh, c), :] + z_dst[0].astype(jnp.float32)
     others = pl.ds(pl.multiple_of((1 - c) * HALF, HALF), HALF)
     gw_buf[:, others] = swapped[...] + z_dst[1].astype(jnp.float32)
-    stores.append(pltpu.make_async_copy(gw_buf, gw_out, store_sem.at[3]))
-    stores[3].start()
+    stores.append(pltpu.make_async_copy(gw_buf, gw_out, store_sem.at[2]))
+    stores[-1].start()
 
     for copy in sent:
         copy.wait_send()
@@ -431,7 +434,7 @@
             pltpu.VMEM((ROWS, FRAG), f32),
             pltpu.VMEM((ROWS, FRAG), f32),
             dma((6,)),
-            dma((4,)),
+            dma((19,)),
             dma((2,)),
             dma((2,)),
             dma((4, 4)),

time: 65 us -> 63.6 us (0.978)
  Pallas kernels: 64.2 us -> 62.8 us
    pallas_call x1, Pallas kernels: 61.8 us -> 60.4 us  [body(): pl.pallas_call(kernel, out_shape=tuple((jax.ShapeDtypeStruct(*shape) for...]
where the time goes in v4:
time: 63.6 us; the launch traced here: 63.4 us
  Pallas kernels  62.8 us (99%)
  between operations  0.64 us (1%)
    pallas_call x1, Pallas kernels, body(): pl.pallas_call(kernel, out_shape=tuple((jax.ShapeDtypeStruct(*shape) for...  60.4 us
    pallas_call x1, Pallas kernels, body(): pl.pallas_call(store, out_shape=tuple((jax.ShapeDtypeStruct(*shape) for s...  2.41 us

profile of v4, /device:TPU:1, one launch (start us, length us, event | category | flops | bytes accessed | tf_op | source)
XLA Modules:
  0.0 63.4 jit_solution(859937292139731064)
XLA Ops:
  0.6 60.4 %up_backward.1 = (bf16[128,6144]{1,0:T(8,128)(2,1)}, f32[96,512]{1,0:T(8,128)}, f32[96,384]{1,0:T(8,128)}, f32[96,384]{1,0:T(8,128)}) custom-call(bf16[128,6144]{1,0:T(8,128)(2,1)} %bitcast.6, bf16[128,512]{1,0:T(8,128)(2,1)} %bitcast.9, bf16[96,512]{1,0:T(8,128)(2,1)} %bitcast.10, bf16[96,384]{1,0:T(8,128)(2,1)} %bitcast.11, f32[96,384]{1,0:T(8,128)} %params.1, ...), custom_call_target="tpu_custom_call" | custom-call | flops 1610612736 | bytes 8388608 | tf_op jit(solution)/shard_map/up_backward/pallas_call | solution.py:404
  61.0 2.4 %store_results.1 = (bf16[128,6144]{1,0:T(8,128)(2,1)}, f32[96,512]{1,0:T(8,128)}, f32[96,384]{1,0:T(8,128)}, f32[96,384]{1,0:T(8,128)}) custom-call(bf16[128,6144]{1,0:T(8,128)(2,1)} %get-tuple-element.12.gi, f32[96,512]{1,0:T(8,128)} %get-tuple-element.13.gw, f32[96,384]{1,0:T(8,128)} %get-tuple-element.14.params, f32[96,384]{1,0:T(8,128)} %get-tuple-element.15.moment), custom_call_target="tpu_custom_call" | custom-call | tf_op jit(solution)/shard_map/store_results/pallas_call | solution.py:467
